TPU v7x, 32 devices: a whole 2x2x4 slice. The times are simulated.
32 devices in a mesh: groups: 2 (over y), gx: 4 (over z), gy: 4 (over x, core).
Axes of the slice: x: 2, y: 2, z: 4, core: 2. Of those that a mesh axis runs over, the one named last changes fastest.
Arguments:
- rows_in: bfloat16 [384, 8192], P(('groups', 'gy'), 'gx'), parts along dimension 0, may hold values from -6 to 6
- gate_weight: bfloat16 [8192, 20480], P('gx', 'gy'), may hold values from -0.09375 to 0.09375
- up_weight: bfloat16 [8192, 20480], P('gx', 'gy'), may hold values from -0.09375 to 0.09375
- down_weight: bfloat16 [20480, 8192], P('gy', 'gx'), may hold values from -0.0625 to 0.0625
- gate_keep: int32 [64, 160], P('gx', 'gy'), may hold values 0 or 1
- up_keep: int32 [64, 160], P('gx', 'gy'), may hold values 0 or 1
- down_keep: int32 [160, 64], P('gy', 'gx'), may hold values 0 or 1
Outputs:
- mixed: bfloat16 [384, 8192], P(('groups', 'gy'), 'gx'), parts along dimension 0
There are 2 independent parts, one for each index of `groups`. A program takes and returns all parts, laid end to end along the dimension named above; an argument that names none is the same for every part. Nothing has to cross between parts.
All inputs are finite; a program needn't handle non-finite values. No bound on the sum of `gate_keep` or of `up_keep` or of `down_keep` on one device may be relied on, other than what follows from the above.
Results may differ from a plain program's by a relative error of at most 0.02.
Values may be sent and summed in bfloat16 or wider, within the bound.
A program may use at most 256 MiB of HBM per device.

v0:
```python
import jax
import jax.numpy as jnp
from jax import lax
from jax.sharding import PartitionSpec as P


def expand_mask(keep_mask, weights):
    tile_size = weights.shape[0] // keep_mask.shape[0]
    outer_rows, outer_cols = keep_mask.shape
    grown = jnp.broadcast_to(
        keep_mask[:, None, :, None], (outer_rows, tile_size, outer_cols, tile_size)
    )
    grown = grown.reshape(outer_rows * tile_size, outer_cols * tile_size)
    return weights * grown.astype(weights.dtype)


def per_device(rows_in, gate_weight, up_weight, down_weight, gate_keep, up_keep, down_keep):
    pruned_gate = expand_mask(gate_keep, gate_weight)
    pruned_up = expand_mask(up_keep, up_weight)
    pruned_down = expand_mask(down_keep, down_weight)
    joined = jnp.concatenate([pruned_gate, pruned_up], axis=1)
    width_half = pruned_gate.shape[1]
    full_rows = lax.all_gather(rows_in, "gy", axis=0, tiled=True)
    picked = full_rows
    summed = lax.psum_scatter(
        jnp.dot(picked, joined, preferred_element_type=jnp.float32).astype(jnp.bfloat16),
        "gx",
        scatter_dimension=0,
        tiled=True,
    ).astype(jnp.float32)
    hidden = (jax.nn.silu(summed[:, :width_half]) * summed[:, width_half:]).astype(jnp.bfloat16)
    hidden_all = lax.all_gather(hidden, "gx", axis=0, tiled=True)
    picked = hidden_all
    return lax.psum_scatter(
        jnp.dot(picked, pruned_down, preferred_element_type=jnp.float32).astype(jnp.bfloat16),
        "gy",
        scatter_dimension=0,
        tiled=True,
    )


def solution(mesh):
    in_specs = (
        P(("groups", "gy"), "gx"),
        P("gx", "gy"),
        P("gx", "gy"),
        P("gy", "gx"),
        P("gx", "gy"),
        P("gx", "gy"),
        P("gy", "gx"),
    )
    out_specs = P(("groups", "gy"), "gx")
    return jax.shard_map(
        per_device, mesh=mesh, in_specs=in_specs, out_specs=out_specs, check_vma=False
    )
```

profile of v0, /device:TPU:1, one launch (start us, length us, event | category | flops | bytes accessed | tf_op | source)
XLA Modules:
  0.0 258.8 jit_solution(2319890351059069515)
XLA Ops:
  6.5 0.0 reduce-scatter.3.cloned.1.call-start
  6.5 0.7 convert_element_type.36
  7.2 0.7 convert_element_type.38
  7.9 10.1 %all_gather.6 = bf16[192,2048]{1,0:T(8,128)(2,1)S(1)} all-gather(bf16[48,2048]{1,0:T(8,128)(2,1)} %param.7), channel_id=1, replica_groups=mesh['groups'=2,'gx'=4,'gy'=4] {'gy'}, dimensions={0}, use_global_device_ids=true | all-gather | bytes 983040 | tf_op jit(solution)/shard_map/all_gather | solution.py:23
  18.1 3.5 %broadcast_in_dim.6 = bf16[16,128,40,128]{3,2,1,0:T(8,128)(2,1)S(1)} broadcast(bf16[16,40]{1,0:T(8,128)(2,1)S(1)} %convert_element_type.36), dimensions={0,2} | broadcast | bytes 20972800 | tf_op jit(solution)/shard_map/broadcast_in_dim | solution.py:10
  21.6 7.5 %broadcast_in_dim.7 = bf16[16,128,40,128]{3,2,1,0:T(8,128)(2,1)} broadcast(bf16[16,40]{1,0:T(8,128)(2,1)S(1)} %convert_element_type.38), dimensions={0,2} | broadcast | bytes 20972800 | tf_op jit(solution)/shard_map/broadcast_in_dim | solution.py:10
  29.1 38.2 %bitcast_multiply_fusion.2 = (bf16[2048,5120]{1,0:T(8,128)(2,1)}, bf16[2048,5120]{1,0:T(8,128)(2,1)}) fusion(bf16[2048,5120]{1,0:T(8,128)(2,1)} %param.9, bf16[256,8,40,128]{3,2,1,0:T(8,128)(2,1)} %bitcast.20, bf16[2048,5120]{1,0:T(8,128)(2,1)} %param.8, bf16[256,8,40,128]{3,2,1,0:T(8,128)(2,1)S(1)} %bitcast.19), kind=kLoop, calls=%fused_computation.7 | loop fusion | flops 20971520 | bytes 125829120 | tf_op jit(solution)/shard_map/mul | solution.py:14
  67.4 0.0 copy-start
  67.4 18.1 %fusion.9 = bf16[192,10240]{1,0:T(8,128)(2,1)} fusion(bf16[192,2048]{1,0:T(8,128)(2,1)S(1)} %all_gather.6, bf16[2048,5120]{1,0:T(8,128)(2,1)} %get-tuple-element.5, bf16[2048,5120]{1,0:T(8,128)(2,1)} %get-tuple-element.6), kind=kOutput, calls=%fused_computation.10 | convolution fusion | flops 8138915840 | bytes 46661632 | tf_op jit(solution)/shard_map/dot_general | solution.py:26
  85.5 0.0 reduce-scatter.3.cloned.1.call-update
  85.5 0.0 all-gather.2.cloned.1.call-start
  85.5 72.8 %reduce-scatter.3.cloned.1.call-done = bf16[48,10240]{1,0:T(8,128)(2,1)} async-done(((bf16[192,10240]{1,0:T(8,128)(2,1)}), bf16[48,10240]{1,0:T(8,128)(2,1)}) %reduce-scatter.3.cloned.1.call-update) | async-done | bytes 983056 | tf_op jit(solution)/shard_map/reduce_scatter | solution.py:25
  158.3 1.3 convert_element_type.42
  159.7 1.0 fusion.13
  160.7 0.0 all-gather.2.cloned.1.call-update
  160.7 0.0 reduce-scatter.5.cloned.1.call-start
  160.8 0.0 copy-done
  160.8 0.1 copy.8
  160.9 44.3 %all-gather.2.cloned.1.call-done = bf16[192,5120]{1,0:T(8,128)(2,1)} async-done(((bf16[48,5120]{1,0:T(8,128)(2,1)}), bf16[192,5120]{1,0:T(8,128)(2,1)}) %all-gather.2.cloned.1.call-update) | async-done | bytes 1966096 | tf_op jit(solution)/shard_map/all_gather | solution.py:32
  205.2 0.0 copy-start.1
  205.2 7.4 %broadcast_in_dim.8 = bf16[40,128,16,128]{3,2,1,0:T(8,128)(2,1)} broadcast(bf16[40,16]{1,0:T(8,128)(2,1)S(1)} %copy.8), dimensions={0,2} | broadcast | bytes 20972800 | tf_op jit(solution)/shard_map/broadcast_in_dim | solution.py:10
  212.5 0.0 copy-done.1
  212.5 17.5 %fusion.12 = bf16[192,2048]{1,0:T(8,128)(2,1)} fusion(bf16[192,5120]{1,0:T(8,128)(2,1)S(1)} %copy-done.1, bf16[5120,2048]{1,0:T(8,128)(2,1)} %param.10, bf16[640,8,16,128]{3,2,1,0:T(8,128)(2,1)} %bitcast.21), kind=kOutput, calls=%fused_computation.11 | convolution fusion | flops 4037410816 | bytes 44695552 | tf_op jit(solution)/shard_map/dot_general | solution.py:35
  230.0 0.0 reduce-scatter.5.cloned.1.call-update
  230.0 22.3 %reduce-scatter.5.cloned.1.call-done = bf16[48,2048]{1,0:T(8,128)(2,1)} async-done(((bf16[192,2048]{1,0:T(8,128)(2,1)}), bf16[48,2048]{1,0:T(8,128)(2,1)}) %reduce-scatter.5.cloned.1.call-update) | async-done | bytes 196624 | tf_op jit(solution)/shard_map/reduce_scatter | solution.py:34
  (1 shorter events, 0.0 us)
Async XLA Ops:
  6.5 151.8 %reduce-scatter.3.cloned.1.call-start = ((), (), s32[]{:S(2)}) async-start(), calls=%async_computation.2 | async-start | bytes 4915200 | tf_op jit(solution)/shard_map/reduce_scatter | solution.py:25
  67.4 93.4 %copy-start = (s32[40,16]{0,1:T(8,128)S(1)}, s32[40,16]{0,1:T(8,128)}, u32[]{:S(2)}) copy-start(s32[40,16]{0,1:T(8,128)} %param.13) | copy-start | bytes 7684
  85.5 119.7 %all-gather.2.cloned.1.call-start = ((), (), s32[]{:S(2)}) async-start(), calls=%async_computation.3 | async-start | bytes 2457600 | tf_op jit(solution)/shard_map/all_gather | solution.py:32
  160.7 91.5 %reduce-scatter.5.cloned.1.call-start = ((), (), s32[]{:S(2)}) async-start(), calls=%async_computation.4 | async-start | bytes 983040 | tf_op jit(solution)/shard_map/reduce_scatter | solution.py:34
  205.2 7.4 %copy-start.1 = (bf16[192,5120]{1,0:T(8,128)(2,1)S(1)}, bf16[192,5120]{1,0:T(8,128)(2,1)}, u32[]{:S(2)}) copy-start(bf16[192,5120]{1,0:T(8,128)(2,1)} %all-gather.2.cloned.1.call-done) | copy-start | bytes 5898244
Sparse Core Ops, SparseCore 0:
  85.6 72.6 reduce-scatter.2
  160.9 44.2 all-gather.1
  230.1 22.0 reduce-scatter.4
where the time goes:
time: 260 us; the launch traced here: 259 us
  waiting for transfers between devices  139 us (53%)
  other arithmetic  42 us (16%)
  matrix products  35.5 us (14%)
  local copies, waits for them, and re-layouts  18.5 us (7%)
  between operations  13.1 us (5%)
  blocking collectives  10.1 us (4%)
    reduce_scatter x1, waiting for transfers between devices, per_device(): lax.psum_scatter(jnp.dot(picked, joined, preferred_element_type=jnp.float...  72.8 us
    all_gather x1, waiting for transfers between devices, per_device(): hidden_all = lax.all_gather(hidden, 'gx', axis=0, tiled=True)  44.3 us
    mul x1, other arithmetic, expand_mask(): return weights * grown.astype(weights.dtype)  38.2 us
    reduce_scatter x1, waiting for transfers between devices, per_device(): lax.psum_scatter(jnp.dot(picked, pruned_down, preferred_element_type=jnp....  22.3 us
    broadcast_in_dim x3, local copies, waits for them, and re-layouts, expand_mask(): jnp.broadcast_to(keep_mask[:, None, :, None], (outer_rows, tile_size, out...  18.4 us
    dot_general x1, matrix products, per_device(): jnp.dot(picked, joined, preferred_element_type=jnp.float32)  18.1 us
    dot_general x1, matrix products, per_device(): jnp.dot(picked, pruned_down, preferred_element_type=jnp.float32)  17.5 us
    all_gather x1, blocking collectives, per_device(): full_rows = lax.all_gather(rows_in, 'gy', axis=0, tiled=True)  10.1 us
  transfers between devices with their start and end apart: 3, of which 3 were waited for; matrix products, arithmetic and copies ran while one was open for 0% of the time, Pallas kernels for 0%

commit v1 on v0

v1 whole, which is shorter than its diff:
```python
import functools

import jax
import jax.numpy as jnp
from jax import lax
from jax.experimental import pallas as pl
from jax.experimental.pallas import tpu as pltpu
from jax.sharding import PartitionSpec as P

BLOCK = 128
CHUNK = 256
SLOTS = 3
SKEW_SUM = 1
SKEW_HID = 1
MESH = pl.DeviceIdType.MESH


def ffn_kernel(
    n, peers, steps_per_way,
    x_ref, gate_ref, up_ref, down_ref, gate_keep, up_keep, down_keep,
    out_ref,
    gathered, rows, weights, down, sums, own, hid, total, leaving, landing,
    row_send, row_recv, row_local, weight_sem, down_sem,
    sum_send, sum_recv, hid_send, hid_recv, out_send, out_recv,
):
    z = lax.axis_index("gx")
    y = lax.axis_index("gy")
    own_rows, depth = x_ref.shape
    all_rows = peers * own_rows
    width = down_ref.shape[1]
    per_way = steps_per_way

    def pos_of(way):
        return jnp.where(way == 0, z, n - 1 - z)

    def onward(way):
        return jnp.where(way == 0, z + 1, z - 1)

    def backward(way):
        return jnp.where(way == 0, z - 1, z + 1)

    def weight_copies(way, j):
        slot = lax.rem(j, SLOTS)
        start = pl.multiple_of((way * per_way + j) * CHUNK, CHUNK)
        return [
            pltpu.make_async_copy(
                source.at[:, pl.ds(start, CHUNK)],
                weights.at[way, slot, :, pl.ds(side * CHUNK, CHUNK)],
                weight_sem.at[way, slot, side],
            )
            for side, source in enumerate((gate_ref, up_ref))
        ]

    def down_copy(way, j):
        start = pl.multiple_of((way * per_way + j) * CHUNK, CHUNK)
        return pltpu.make_async_copy(
            down_ref.at[pl.ds(start, CHUNK), :], down.at[way, j], down_sem.at[way, j]
        )

    def sum_copy(way, j):
        return pltpu.make_async_remote_copy(
            sums.at[way, j], sums.at[way, j], sum_send.at[way, j], sum_recv.at[way, j],
            device_id={"gx": onward(way)}, device_id_type=MESH,
        )

    def hid_copy(way, j):
        return pltpu.make_async_remote_copy(
            hid.at[way, j], hid.at[way, j], hid_send.at[way, j], hid_recv.at[way, j],
            device_id={"gx": backward(way)}, device_id_type=MESH,
        )

    def row_copy(sender, receiver):
        return pltpu.make_async_remote_copy(
            x_ref, gathered.at[sender], row_send.at[receiver], row_recv.at[sender],
            device_id={"gy": receiver}, device_id_type=MESH,
        )

    def out_copy(sender, receiver):
        return pltpu.make_async_remote_copy(
            leaving.at[receiver], landing.at[sender], out_send.at[receiver], out_recv.at[sender],
            device_id={"gy": receiver}, device_id_type=MESH,
        )

    barrier = pltpu.get_barrier_semaphore()
    for step in range(1, peers):
        pl.semaphore_signal(
            barrier, inc=1, device_id={"gy": lax.rem(y + step, peers)}, device_id_type=MESH
        )

    @pl.when(z > 0)
    def _():
        pl.semaphore_signal(barrier, inc=1, device_id={"gx": z - 1}, device_id_type=MESH)

    @pl.when(z < n - 1)
    def _():
        pl.semaphore_signal(barrier, inc=1, device_id={"gx": z + 1}, device_id_type=MESH)

    local = pltpu.make_async_copy(x_ref, gathered.at[y], row_local)
    local.start()
    for way in range(2):
        for j in range(min(SLOTS, per_way)):
            for copy in weight_copies(way, j):
                copy.start()
    pl.semaphore_wait(barrier, peers - 1 + jnp.where(z > 0, 1, 0) + jnp.where(z < n - 1, 1, 0))

    for step in range(1, peers):
        row_copy(y, lax.rem(y + step, peers)).start()
    local.wait()
    total[...] = jnp.zeros_like(total)
    for step in range(1, peers):
        row_copy(lax.rem(y + step, peers), y).wait_recv()
    if own_rows % 16 == 0:
        for part in range(peers):
            rows[part * own_rows:(part + 1) * own_rows, :] = gathered[part]
    else:
        rows[...] = jnp.concatenate(
            [gathered[part].astype(jnp.float32) for part in range(peers)], axis=0
        ).astype(rows.dtype)

    def mask_tile(keep):
        return jnp.full((16, BLOCK), keep.astype(jnp.float32)).astype(jnp.bfloat16)

    def masked(tile, keep):
        return (tile.reshape(BLOCK // 16, 16, BLOCK) * mask_tile(keep)[None]).reshape(BLOCK, BLOCK)

    blocks = CHUNK // BLOCK

    def partial_sums(s, way):
        pos = pos_of(way)
        j = s - SKEW_SUM * pos

        @pl.when((j >= 0) & (j < per_way))
        def _():
            slot = lax.rem(j, SLOTS)
            for copy in weight_copies(way, j):
                copy.wait()
            first = (way * per_way + j) * blocks

            @pl.loop(0, depth // BLOCK)
            def _(k):
                top = pl.multiple_of(k * BLOCK, BLOCK)
                for side, keeps in enumerate((gate_keep, up_keep)):
                    for b in range(blocks):
                        lanes = slice((side * blocks + b) * BLOCK, (side * blocks + b + 1) * BLOCK)
                        weights[way, slot, pl.ds(top, BLOCK), lanes] = masked(
                            weights[way, slot, pl.ds(top, BLOCK), lanes], keeps[k, first + b]
                        )

            own[way] = jnp.dot(
                rows[...], weights[way, slot], preferred_element_type=jnp.float32
            )

            @pl.when(j + SLOTS < per_way)
            def _():
                for copy in weight_copies(way, j + SLOTS):
                    copy.start()

    def pass_sums(s, way):
        pos = pos_of(way)
        j = s - SKEW_SUM * pos

        @pl.when((j >= 0) & (j < per_way))
        def _():
            @pl.when(pos == 0)
            def _():
                sums[way, j] = own[way].astype(jnp.bfloat16)

            @pl.when(pos > 0)
            def _():
                sum_copy(way, j).wait_recv()

            @pl.when((pos > 0) & (pos < n - 1))
            def _():
                sums[way, j] = (sums[way, j].astype(jnp.float32) + own[way]).astype(jnp.bfloat16)

            @pl.when(pos < n - 1)
            def _():
                sum_copy(way, j).start()

            @pl.when(pos == n - 1)
            def _():
                gate = sums[way, j, :, :CHUNK].astype(jnp.float32) + own[way, :, :CHUNK]
                up = sums[way, j, :, CHUNK:].astype(jnp.float32) + own[way, :, CHUNK:]
                hid[way, j] = (gate / (1.0 + jnp.exp(-gate)) * up).astype(jnp.bfloat16)

    def hid_index(s, pos):
        return s - SKEW_SUM * (n - 1) - SKEW_HID * (n - 1 - pos)

    def pass_hidden(s, way):
        pos = pos_of(way)
        j = hid_index(s, pos)

        @pl.when((j >= 0) & (j < per_way))
        def _():
            @pl.when(pos < n - 1)
            def _():
                hid_copy(way, j).wait_recv()

            @pl.when(pos > 0)
            def _():
                hid_copy(way, j).start()

    def mix(s, way):
        pos = pos_of(way)
        j = hid_index(s, pos)

        @pl.when((j >= 0) & (j < per_way))
        def _():
            down_copy(way, j).wait()
            first = (way * per_way + j) * blocks
            span = min(256, width)

            @pl.loop(0, width // span)
            def _(c):
                for q in range(span // BLOCK):
                    lanes = pl.ds(pl.multiple_of(c * span + q * BLOCK, BLOCK), BLOCK)
                    for b in range(blocks):
                        down[way, j, b * BLOCK:(b + 1) * BLOCK, lanes] = masked(
                            down[way, j, b * BLOCK:(b + 1) * BLOCK, lanes],
                            down_keep[first + b, c * (span // BLOCK) + q],
                        )
                lanes = pl.ds(pl.multiple_of(c * span, BLOCK), span)
                total[:, lanes] += jnp.dot(
                    hid[way, j], down[way, j, :, lanes], preferred_element_type=jnp.float32
                )

    def fetch_down(s, way):
        @pl.when(s < per_way)
        def _():
            down_copy(way, s).start()

    last = per_way + (SKEW_SUM + SKEW_HID) * (n - 1)

    @pl.loop(0, last)
    def _(s):
        for part in (partial_sums, pass_sums, pass_hidden, fetch_down, mix):
            @pl.loop(0, 2)
            def _(way):
                part(s, way)

    for step in range(1, peers):
        who = lax.rem(y + step, peers)
        leaving[who] = total[pl.ds(pl.multiple_of(who * own_rows, 8), own_rows), :].astype(jnp.bfloat16)
        out_copy(y, who).start()

    for step in range(1, peers):
        row_copy(y, lax.rem(y + step, peers)).wait_send()

    @pl.loop(0, per_way)
    def _(j):
        @pl.loop(0, 2)
        def _(way):
            pos = pos_of(way)

            @pl.when(pos < n - 1)
            def _():
                sum_copy(way, j).wait_send()

            @pl.when(pos > 0)
            def _():
                hid_copy(way, j).wait_send()

    result = total[pl.ds(pl.multiple_of(y * own_rows, 8), own_rows), :]
    for step in range(1, peers):
        who = lax.rem(y + step, peers)
        out_copy(who, y).wait_recv()
        result = result + landing[who].astype(jnp.float32)
    out_ref[...] = result.astype(out_ref.dtype)
    for step in range(1, peers):
        out_copy(y, lax.rem(y + step, peers)).wait_send()


def per_device(n, peers, rows_in, gate_weight, up_weight, down_weight, gate_keep, up_keep, down_keep):
    own_rows, depth = rows_in.shape
    all_rows = own_rows * peers
    hidden, width = down_weight.shape
    per_way = hidden // CHUNK // 2
    bf16, f32 = jnp.bfloat16, jnp.float32
    dma = pltpu.SemaphoreType.DMA
    hbm = pl.BlockSpec(memory_space=pl.ANY)
    smem = pl.BlockSpec(memory_space=pltpu.SMEM)
    return pl.pallas_call(
        functools.partial(ffn_kernel, n, peers, per_way),
        out_shape=jax.ShapeDtypeStruct((own_rows, width), bf16),
        in_specs=[hbm] * 4 + [smem] * 3,
        out_specs=pl.BlockSpec(memory_space=pltpu.VMEM),
        scratch_shapes=[
            pltpu.VMEM((peers, own_rows, depth), bf16),
            pltpu.VMEM((all_rows, depth), bf16),
            pltpu.VMEM((2, SLOTS, depth, 2 * CHUNK), bf16),
            pltpu.VMEM((2, per_way, CHUNK, width), bf16),
            pltpu.VMEM((2, per_way, all_rows, 2 * CHUNK), bf16),
            pltpu.VMEM((2, all_rows, 2 * CHUNK), f32),
            pltpu.VMEM((2, per_way, all_rows, CHUNK), bf16),
            pltpu.VMEM((all_rows, width), f32),
            pltpu.VMEM((peers, own_rows, width), bf16),
            pltpu.VMEM((peers, own_rows, width), bf16),
            dma((peers,)), dma((peers,)), dma,
            dma((2, SLOTS, 2)), dma((2, per_way)),
            dma((2, per_way)), dma((2, per_way)),
            dma((2, per_way)), dma((2, per_way)),
            dma((peers,)), dma((peers,)),
        ],
        compiler_params=pltpu.CompilerParams(
            collective_id=0, has_side_effects=True, vmem_limit_bytes=58 * 1024 * 1024
        ),
    )(rows_in, gate_weight, up_weight, down_weight, gate_keep, up_keep, down_keep)


def solution(mesh):
    in_specs = (
        P(("groups", "gy"), "gx"),
        P("gx", "gy"),
        P("gx", "gy"),
        P("gy", "gx"),
        P("gx", "gy"),
        P("gx", "gy"),
        P("gy", "gx"),
    )
    out_specs = P(("groups", "gy"), "gx")
    body = functools.partial(per_device, mesh.shape["gx"], mesh.shape["gy"])
    return jax.shard_map(body, mesh=mesh, in_specs=in_specs, out_specs=out_specs, check_vma=False)
```

time: 260 us -> 117 us (0.45)
  waiting for transfers between devices: 139 us -> 0 us
  Pallas kernels: 0 us -> 114 us
  other arithmetic: 42 us -> 0 us
  matrix products: 35.5 us -> 0 us
  local copies, waits for them, and re-layouts: 18.5 us -> 3 us
  between operations: 13.1 us -> 0.01 us
  blocking collectives: 10.1 us -> 0 us
    pallas_call x0 -> x1, Pallas kernels: none -> 114 us  [per_device(): pl.pallas_call(functools.partial(ffn_kernel, n, peers, per_way), out_shap...]
    reduce_scatter x2 -> x0, waiting for transfers between devices: 95.1 us -> none  [the longest x1 72.8 us: per_device(): lax.psum_scatter(jnp.dot(picked, joined, preferred_element_type=jnp.float...]
    all_gather x1 -> x0, waiting for transfers between devices: 44.3 us -> none  [per_device(): hidden_all = lax.all_gather(hidden, 'gx', axis=0, tiled=True)]
    mul x1 -> x0, other arithmetic: 38.2 us -> none  [expand_mask(): return weights * grown.astype(weights.dtype)]
    dot_general x2 -> x0, matrix products: 35.5 us -> none  [the longest x1 18.1 us: per_device(): jnp.dot(picked, joined, preferred_element_type=jnp.float32)]
    broadcast_in_dim x3 -> x0, local copies, waits for them, and re-layouts: 18.4 us -> none  [expand_mask(): jnp.broadcast_to(keep_mask[:, None, :, None], (outer_rows, tile_size, out...]
    all_gather x1 -> x0, blocking collectives: 10.1 us -> none  [per_device(): full_rows = lax.all_gather(rows_in, 'gy', axis=0, tiled=True)]
    convert_element_type x5 -> x0, other arithmetic: 3.78 us -> none  [the longest x3 1.4 us: expand_mask(): return weights * grown.astype(weights.dtype)]
  transfers between devices with their start and end apart: 3 -> 0, of which waited for: 3 -> 0; matrix products, arithmetic and copies ran while one was open for 0% -> 0% of each run, Pallas kernels for 0% -> 0%
where the time goes in v1:
time: 117 us
  Pallas kernels  114 us (97%)
  local copies, waits for them, and re-layouts  3 us (3%)
    pallas_call x1, Pallas kernels, per_device(): pl.pallas_call(functools.partial(ffn_kernel, n, peers, per_way), out_shap...  114 us
    unnamed x2, local copies, waits for them, and re-layouts  3 us

profile of v1, /device:TPU:1, one launch (start us, length us, event | category | flops | bytes accessed | tf_op | source)
XLA Modules:
  0.0 116.9 jit_solution(16080965865521436586)
XLA Ops:
  0.0 1.4 %copy.8.down_keep = s32[40,16]{1,0:T(8,128)} copy(s32[40,16]{0,1:T(8,128)} %param.13) | data formatting | bytes 5120 | tf_op args[6]
  1.4 113.9 %shard_map.73 = bf16[48,2048]{1,0:T(8,128)(2,1)} custom-call(bf16[48,2048]{1,0:T(8,128)(2,1)} %x_ref.1, bf16[2048,5120]{1,0:T(8,128)(2,1)} %gate_ref.1, bf16[2048,5120]{1,0:T(8,128)(2,1)} %up_ref.1, bf16[5120,2048]{1,0:T(8,128)(2,1)} %down_ref.1, s32[16,40]{1,0:T(8,128)} %gate_keep.1, s32[16,40]{1,0:T(8,128)} %up_keep.1, s32[40,16]{1,0:T(8,128)} %copy.8.down_keep), custom_call_target="tpu_custom_call" | custom-call | tf_op jit(solution)/shard_map/pallas_call | solution.py:282
  115.3 1.6 %copy.10 = bf16[48,2048]{1,0:T(8,128)(2,1)} copy(bf16[48,2048]{1,0:T(8,128)(2,1)} %shard_map.73) | data formatting | bytes 393216

commit v2 on v1

--- a/solution.py
+++ b/solution.py
@@ -8,10 +8,10 @@
 from jax.sharding import PartitionSpec as P
 
 BLOCK = 128
-CHUNK = 256
-SLOTS = 3
-SKEW_SUM = 1
-SKEW_HID = 1
+CHUNK = 128
+SLOTS = 4
+SKEW_SUM = 2
+SKEW_HID = 2
 MESH = pl.DeviceIdType.MESH
 
 
@@ -136,7 +136,7 @@
                 copy.wait()
             first = (way * per_way + j) * blocks
 
-            @pl.loop(0, depth // BLOCK)
+            @pl.loop(0, depth // BLOCK, unroll=min(4, depth // BLOCK))
             def _(k):
                 top = pl.multiple_of(k * BLOCK, BLOCK)
                 for side, keeps in enumerate((gate_keep, up_keep)):
@@ -208,21 +208,16 @@
         def _():
             down_copy(way, j).wait()
             first = (way * per_way + j) * blocks
-            span = min(256, width)
-
-            @pl.loop(0, width // span)
+
+            @pl.loop(0, width // BLOCK, unroll=min(4, width // BLOCK))
             def _(c):
-                for q in range(span // BLOCK):
-                    lanes = pl.ds(pl.multiple_of(c * span + q * BLOCK, BLOCK), BLOCK)
-                    for b in range(blocks):
-                        down[way, j, b * BLOCK:(b + 1) * BLOCK, lanes] = masked(
-                            down[way, j, b * BLOCK:(b + 1) * BLOCK, lanes],
-                            down_keep[first + b, c * (span // BLOCK) + q],
-                        )
-                lanes = pl.ds(pl.multiple_of(c * span, BLOCK), span)
-                total[:, lanes] += jnp.dot(
-                    hid[way, j], down[way, j, :, lanes], preferred_element_type=jnp.float32
-                )
+                lanes = pl.ds(pl.multiple_of(c * BLOCK, BLOCK), BLOCK)
+                for b in range(blocks):
+                    down[way, j, b * BLOCK:(b + 1) * BLOCK, lanes] = masked(
+                        down[way, j, b * BLOCK:(b + 1) * BLOCK, lanes], down_keep[c, first + b]
+                    )
+
+            total[...] += jnp.dot(hid[way, j], down[way, j], preferred_element_type=jnp.float32)
 
     def fetch_down(s, way):
         @pl.when(s < per_way)
@@ -304,7 +299,7 @@
         compiler_params=pltpu.CompilerParams(
             collective_id=0, has_side_effects=True, vmem_limit_bytes=58 * 1024 * 1024
         ),
-    )(rows_in, gate_weight, up_weight, down_weight, gate_keep, up_keep, down_keep)
+    )(rows_in, gate_weight, up_weight, down_weight, gate_keep, up_keep, down_keep.T)
 
 
 def solution(mesh):

time: 117 us -> 104 us (0.89)
  Pallas kernels: 114 us -> 102 us
  local copies, waits for them, and re-layouts: 3 us -> 1.62 us
    pallas_call x1, Pallas kernels: 114 us -> 102 us  [per_device(): pl.pallas_call(functools.partial(ffn_kernel, n, peers, per_way), out_shap...]
    unnamed x2 -> x1, local copies, waits for them, and re-layouts: 3 us -> 1.62 us
where the time goes in v2:
time: 104 us
  Pallas kernels  102 us (98%)
  local copies, waits for them, and re-layouts  1.62 us (2%)
    pallas_call x1, Pallas kernels, per_device(): pl.pallas_call(functools.partial(ffn_kernel, n, peers, per_way), out_shap...  102 us

profile of v2, /device:TPU:1, one launch (start us, length us, event | category | flops | bytes accessed | tf_op | source)
XLA Modules:
  0.0 103.7 jit_solution(15616527490888261789)
XLA Ops:
  0.0 102.1 %shard_map.73 = bf16[48,2048]{1,0:T(8,128)(2,1)} custom-call(bf16[48,2048]{1,0:T(8,128)(2,1)} %x_ref.1, bf16[2048,5120]{1,0:T(8,128)(2,1)} %gate_ref.1, bf16[2048,5120]{1,0:T(8,128)(2,1)} %up_ref.1, bf16[5120,2048]{1,0:T(8,128)(2,1)} %down_ref.1, s32[16,40]{1,0:T(8,128)} %gate_keep.1, s32[16,40]{1,0:T(8,128)} %up_keep.1, s32[16,40]{1,0:T(8,128)} %bitcast.1), custom_call_target="tpu_custom_call" | custom-call | tf_op jit(solution)/shard_map/pallas_call | solution.py:277
  102.1 1.6 %copy.9 = bf16[48,2048]{1,0:T(8,128)(2,1)} copy(bf16[48,2048]{1,0:T(8,128)(2,1)} %shard_map.73) | data formatting | bytes 393216
